TPU v7x, 32 devices: a whole 2x2x4 slice. The times are simulated.
32 devices in a mesh: shard: 8 (over z, y), tensor: 4 (over x, core).
Axes of the slice: x: 2, y: 2, z: 4, core: 2. Of those that a mesh axis runs over, the one named last changes fastest.
Arguments:
- grad_query: bfloat16 [8, 1024, 512], P('shard', None, 'tensor'), may hold values from -8 to 8
- error_query: float32 [8, 1024, 512], P('shard', None, 'tensor'), may hold values from -3 to 3
- grad_output: bfloat16 [8, 512, 1024], P('shard', 'tensor'), may hold values from -8 to 8
- error_output: float32 [8, 512, 1024], P('shard', 'tensor'), may hold values from -3 to 3
- start_query: float32 [512, 32], P('tensor'), may hold values from -6 to 6
- start_output: float32 [1024, 32], replicated, may hold values from -6 to 6
- weight_query: float32 [1024, 512], P('shard', 'tensor'), may hold values from -0.1875 to 0.1875
- weight_output: float32 [512, 1024], P('tensor', 'shard'), may hold values from -0.25 to 0.25
- moment_query: float32 [1024, 512], P('shard', 'tensor'), may hold values from -1.2 to 1.2
- moment_output: float32 [512, 1024], P('tensor', 'shard'), may hold values from -1.2 to 1.2
- grad_vector: bfloat16 [8, 3584], P('shard'), may hold values from -12 to 12
- moment_vector: float32 [3584], P('shard'), may hold values from -1.2 to 1.2
- weight_vector: float32 [3584], P('shard'), may hold values from 0.5 to 1.5
Outputs:
- new_error_query: float32 [8, 1024, 512], P('shard', None, 'tensor')
- new_error_output: float32 [8, 512, 1024], P('shard', 'tensor')
- new_moment_query: float32 [1024, 512], P('shard', 'tensor')
- new_moment_output: float32 [512, 1024], P('tensor', 'shard')
- new_weight_query: float32 [1024, 512], P(None, 'tensor')
- new_weight_output: float32 [512, 1024], P('tensor')
- new_moment_vector: float32 [3584], P('shard')
- new_weight_vector: float32 [3584], replicated
All inputs are finite; a program needn't handle non-finite values.
Results may differ from a plain program's by a relative error of at most 0.0003.
Values sent between devices are 32-bit elements; how exact they have to be, the bound alone decides.
A program may use at most 64 MiB of HBM per device.

v0:
```python
import jax
import jax.numpy as jnp
from jax import lax
from jax.sharding import PartitionSpec as P

ROUNDS = 2


highest = lax.Precision.HIGHEST


def product(left, right):
    return jnp.dot(left, right, precision=highest, preferred_element_type=jnp.float32)


def product_inner(left, right):
    return lax.dot_general(
        left, right, (((0,), (0,)), ((), ())), precision=highest, preferred_element_type=jnp.float32
    )


def solve_rows(gram, factor):
    lower = jnp.linalg.cholesky(gram)
    return jax.scipy.linalg.solve_triangular(lower, factor.T, lower=True).T


def orthonormal(factor):
    return solve_rows(product_inner(factor, factor), factor)


def orthonormal_rows(factor):
    gram = lax.psum(product_inner(factor, factor), "tensor")
    return solve_rows(gram, factor)


def local(
    grad_query,
    error_query,
    grad_output,
    error_output,
    start_query,
    start_output,
    weight_query,
    weight_output,
    moment_query,
    moment_output,
    grad_vector,
    moment_vector,
    weight_vector,
):
    replicas = lax.axis_size("shard")
    shard_index = lax.axis_index("shard")
    total_query = grad_query[0].astype(jnp.float32) + error_query[0]
    total_output = grad_output[0].astype(jnp.float32) + error_output[0]
    factor_query = start_query
    factor_output = start_output
    for turn in range(ROUNDS):
        part_query = product(total_query, factor_query)
        part_output = product(total_output, factor_output)
        sum_query = lax.psum(part_query, ("shard", "tensor"))
        sum_output = lax.psum(part_output, "shard")
        left_query = orthonormal(sum_query)
        left_output = orthonormal_rows(sum_output)
        right_query_part = product_inner(total_query, left_query)
        right_output_part = product_inner(total_output, left_output)
        factor_query = lax.psum(right_query_part, "shard")
        factor_output = lax.psum(right_output_part, ("shard", "tensor"))
    approx_query = product(left_query, factor_query.T) / replicas
    approx_output = product(left_output, factor_output.T) / replicas
    new_error_query = (total_query - approx_query)[None]
    new_error_output = (total_output - approx_output)[None]
    rows_block = moment_query.shape[0]
    block_query = lax.dynamic_slice_in_dim(approx_query, shard_index * rows_block, rows_block, 0)
    cols_block = moment_output.shape[1]
    block_output = lax.dynamic_slice_in_dim(approx_output, shard_index * cols_block, cols_block, 1)
    new_moment_query = 0.9 * moment_query + block_query
    new_moment_output = 0.9 * moment_output + block_output
    stepped_query = weight_query - 0.01 * new_moment_query
    stepped_output = weight_output - 0.01 * new_moment_output
    local_vector = grad_vector[0].astype(jnp.float32)
    vector_block = moment_vector.shape[0]
    vector_whole = lax.psum(local_vector, "shard")
    vector_part = lax.dynamic_slice_in_dim(
        vector_whole, shard_index * vector_block, vector_block, 0
    )
    vector_mean = vector_part / replicas
    new_moment_vector = 0.9 * moment_vector + vector_mean
    stepped_vector = weight_vector - 0.01 * new_moment_vector
    new_weight_query, new_weight_output, new_weight_vector = (
        lax.all_gather(stepped_query, "shard", axis=0, tiled=True),
        lax.all_gather(stepped_output, "shard", axis=1, tiled=True),
        lax.all_gather(stepped_vector, "shard", axis=0, tiled=True),
    )
    return (
        new_error_query,
        new_error_output,
        new_moment_query,
        new_moment_output,
        new_weight_query,
        new_weight_output,
        new_moment_vector,
        new_weight_vector,
    )


def solution(mesh):
    in_specs = (
        P("shard", None, "tensor"),
        P("shard", None, "tensor"),
        P("shard", "tensor", None),
        P("shard", "tensor", None),
        P("tensor", None),
        P(),
        P("shard", "tensor"),
        P("tensor", "shard"),
        P("shard", "tensor"),
        P("tensor", "shard"),
        P("shard", None),
        P("shard"),
        P("shard"),
    )
    out_specs = (
        P("shard", None, "tensor"),
        P("shard", "tensor", None),
        P("shard", "tensor"),
        P("tensor", "shard"),
        P(None, "tensor"),
        P("tensor", None),
        P("shard"),
        P(),
    )
    return jax.shard_map(local, mesh=mesh, in_specs=in_specs, out_specs=out_specs, check_vma=False)
```

profile of v0, /device:TPU:0, one launch (start us, length us, event | category | flops | bytes accessed | tf_op | source)
XLA Modules:
  0.0 512.4 jit_solution(1252998687482371478)
XLA Ops:
  8.1 1.7 fusion.6
  9.8 39.0 %psum.81 = f32[128,32]{0,1:T(8,128)S(1)} all-reduce(f32[128,32]{0,1:T(8,128)S(1)} %fusion.6), channel_id=1, replica_groups=mesh['shard'=8,'tensor'=4] {'shard'}, use_global_device_ids=true, to_apply=%region_6.9 | all-reduce | flops 4096 | bytes 32768 | tf_op jit(solution)/shard_map/psum | solution.py:61
  48.9 10.1 %psum.82 = f32[32,32]{0,1:T(8,128)S(1)} all-reduce(f32[32,32]{0,1:T(8,128)S(1)} %fusion.42), channel_id=1, replica_groups=mesh['shard'=8,'tensor'=4] {'tensor'}, use_global_device_ids=true, to_apply=%region_7.10 | all-reduce | flops 1024 | bytes 8192 | tf_op jit(solution)/shard_map/psum | solution.py:32
  59.1 2.9 cholesky.96
  63.4 2.5 custom-call.12
  66.1 1.8 fusion.4
  67.9 1.3 fusion.15
  71.3 124.5 %all-reduce.10.cloned.1.call-done = (f32[1024,32]{0,1:T(8,128)}, f32[1024,32]{1,0:T(8,128)}) async-done(((f32[1024,32]{0,1:T(8,128)}, f32[1024,32]{1,0:T(8,128)}), (f32[1024,32]{0,1:T(8,128)}, f32[1024,32]{1,0:T(8,128)})) %all-reduce.10.cloned.1.call-update) | async-done | bytes 262160 | tf_op jit(solution)/shard_map/psum | solution.py:60
  195.8 2.0 fusion.2
  198.2 2.9 cholesky.74
  202.4 2.4 custom-call.10
  206.2 37.1 %all-reduce.4 = (f32[128,32]{1,0:T(8,128)S(1)}, f32[128,32]{0,1:T(8,128)S(1)}, f32[3584]{0:T(1024)S(1)}) all-reduce(f32[128,32]{1,0:T(8,128)S(1)} %fusion.13, f32[128,32]{0,1:T(8,128)S(1)} %fusion.2, f32[3584]{0:T(1024)S(1)} %convert_reduce_fusion), channel_id=1, replica_groups=mesh['shard'=8,'tensor'=4] {'shard'}, use_global_device_ids=true, to_apply=%region_3.6 | all-reduce | flops 11776 | bytes 94208 | tf_op jit(solution)/shard_map/psum | solution.py:66
  243.5 10.2 %psum.85 = f32[32,32]{0,1:T(8,128)S(1)} all-reduce(f32[32,32]{0,1:T(8,128)S(1)} %fusion.43), channel_id=1, replica_groups=mesh['shard'=8,'tensor'=4] {'tensor'}, use_global_device_ids=true, to_apply=%region_10.0 | all-reduce | flops 1024 | bytes 8192 | tf_op jit(solution)/shard_map/psum | solution.py:32
  253.8 2.9 cholesky.107
  258.1 2.5 custom-call.13
  260.7 1.3 fusion.11
  262.1 1.8 fusion
  265.2 124.0 %all-reduce.8.cloned.1.call-done = (f32[1024,32]{0,1:T(8,128)}, f32[1024,32]{1,0:T(8,128)}) async-done(((f32[1024,32]{0,1:T(8,128)}, f32[1024,32]{1,0:T(8,128)}), (f32[1024,32]{0,1:T(8,128)}, f32[1024,32]{1,0:T(8,128)})) %all-reduce.8.cloned.1.call-update) | async-done | bytes 262160 | tf_op jit(solution)/shard_map/psum | solution.py:60
  389.3 1.7 convolution_multiply_fusion.1
  391.3 2.9 cholesky.85
  395.6 2.4 custom-call.11
  400.3 37.5 %all-reduce.3 = (f32[128,32]{1,0:T(8,128)S(1)}, f32[3584]{0:T(1024)}) all-reduce(f32[128,32]{1,0:T(8,128)S(1)} %fusion.9, f32[3584]{0:T(1024)S(1)} %get-tuple-element.24), channel_id=1, replica_groups=mesh['shard'=8,'tensor'=4] {'shard'}, use_global_device_ids=true, to_apply=%region_5.8 | all-reduce | flops 7680 | bytes 61440 | tf_op jit(solution)/shard_map/psum | solution.py:66
  440.3 31.8 %all_gather.9 = f32[1024,128]{1,0:T(8,128)S(1)} all-gather(f32[128,128]{1,0:T(8,128)S(1)} %get-tuple-element.22), channel_id=1, replica_groups=mesh['shard'=8,'tensor'=4] {'shard'}, dimensions={0}, use_global_device_ids=true | all-gather | bytes 589824 | tf_op jit(solution)/shard_map/all_gather | solution.py:90
  472.8 31.2 %all_gather.10 = f32[128,1024]{1,0:T(8,128)S(1)} all-gather(f32[128,128]{1,0:T(8,128)S(1)} %get-tuple-element.20), channel_id=1, replica_groups=mesh['shard'=8,'tensor'=4] {'shard'}, dimensions={1}, use_global_device_ids=true | all-gather | bytes 589824 | tf_op jit(solution)/shard_map/all_gather | solution.py:91
  (77 shorter events, 18.8 us)
Async XLA Ops:
  7.2 0.9 copy-start
  7.2 58.9 %copy-start.1 = (f32[1,128,1024]{2,1,0:T(8,128)S(1)}, f32[1,128,1024]{2,1,0:T(8,128)}, u32[]{:S(2)}) copy-start(f32[1,128,1024]{2,1,0:T(8,128)} %param.21) | copy-start | bytes 1572868
  7.2 188.6 %all-reduce.10.cloned.1.call-start = ((), (), s32[]{:S(2)}) async-start(), calls=%async_computation.1 | async-start | bytes 1310720 | tf_op jit(solution)/shard_map/psum | solution.py:60
  9.8 56.3 %copy-start.3 = (bf16[1,128,1024]{2,1,0:T(8,128)(2,1)S(1)}, bf16[1,128,1024]{2,1,0:T(8,128)(2,1)}, u32[]{:S(2)}) copy-start(bf16[1,128,1024]{2,1,0:T(8,128)(2,1)} %param.20) | copy-start | bytes 786436
  66.1 1.8 copy-start.2
  66.1 1.8 copy-start.4
  66.1 1.8 copy-start.11
  69.3 320.0 %all-reduce.8.cloned.1.call-start = ((), (), s32[]{:S(2)}) async-start(), calls=%async_computation | async-start | bytes 1310720 | tf_op jit(solution)/shard_map/psum | solution.py:60
  69.3 1.9 copy-start.12
  69.3 0.7 copy-start.15
  195.8 2.0 copy-start.5
  263.9 0.7 copy-start.13
  263.9 0.7 copy-start.14
  389.3 1.7 copy-start.6
  438.8 0.9 copy-start.7
  438.8 0.9 copy-start.8
  440.3 31.9 %copy-start.9 = (f32[128,128]{1,0:T(8,128)S(1)}, f32[128,128]{1,0:T(8,128)}, u32[]{:S(2)}) copy-start(f32[128,128]{1,0:T(8,128)} %param.25) | copy-start | bytes 196612
  440.3 31.9 %copy-start.10 = (f32[128,128]{1,0:T(8,128)S(1)}, f32[128,128]{1,0:T(8,128)}, u32[]{:S(2)}) copy-start(f32[128,128]{1,0:T(8,128)} %param.27) | copy-start | bytes 196612
Sparse Core Ops, SparseCore 0:
  69.4 126.3 all-reduce.9
  264.0 125.2 all-reduce.7
where the time goes:
time: 513 us; the launch traced here: 512 us
  waiting for transfers between devices  249 us (49%)
  blocking collectives  197 us (38%)
  other arithmetic  30.5 us (6%)
  matrix products  16.5 us (3%)
  between operations  15 us (3%)
    psum x2, waiting for transfers between devices, local(): sum_query = lax.psum(part_query, ('shard', 'tensor'))  249 us
    psum x2, blocking collectives, local(): factor_query = lax.psum(right_query_part, 'shard')  74.6 us
    psum x1, blocking collectives, local(): sum_output = lax.psum(part_output, 'shard')  39 us
    all_gather x1, blocking collectives, local(): lax.all_gather(stepped_query, 'shard', axis=0, tiled=True)  31.8 us
    all_gather x1, blocking collectives, local(): lax.all_gather(stepped_output, 'shard', axis=1, tiled=True)  31.2 us
    psum x2, blocking collectives, orthonormal_rows(): gram = lax.psum(product_inner(factor, factor), 'tensor')  20.3 us
    another operation x12, other arithmetic, solve_rows(): lower = jnp.linalg.cholesky(gram)  14.4 us
    another operation x8, other arithmetic, solve_rows(): return jax.scipy.linalg.solve_triangular(lower, factor.T, lower=True).T  12.4 us
  transfers between devices with their start and end apart: 2, of which 2 were waited for; matrix products, arithmetic and copies ran while one was open for 0% of the time, Pallas kernels for 0%

commit v1 on v0

--- a/solution.py
+++ b/solution.py
@@ -1,6 +1,8 @@
 import jax
 import jax.numpy as jnp
 from jax import lax
+from jax.experimental import pallas as pl
+from jax.experimental.pallas import tpu as pltpu
 from jax.sharding import PartitionSpec as P
 
 ROUNDS = 2
@@ -103,6 +105,258 @@
     )
 
 
+Z, Y, TENSOR = 4, 2, 4
+SHARD = Z * Y
+RANK = 32
+B = 128
+VEC_PAD = 512
+SLOTS = 128
+f32 = jnp.float32
+
+
+def nn(left, right):
+    return lax.dot_general(left, right, (((1,), (0,)), ((), ())), precision=highest, preferred_element_type=f32)
+
+
+def nt(left, right):
+    return lax.dot_general(left, right, (((1,), (1,)), ((), ())), precision=highest, preferred_element_type=f32)
+
+
+def inverse_lower(gram):
+    row = lax.broadcasted_iota(jnp.int32, (RANK, RANK), 0)
+    lane = lax.broadcasted_iota(jnp.int32, (RANK, RANK), 1)
+    left, right = gram, (row == lane).astype(f32)
+    row_of = lax.broadcasted_iota(jnp.int32, (RANK, 1), 0)
+    for k in range(RANK):
+        ratio = jnp.where(row_of > k, left[:, k : k + 1] * (1.0 / left[k : k + 1, k : k + 1]), 0.0)
+        left, right = left - ratio * left[k : k + 1, :], right - ratio * right[k : k + 1, :]
+    diagonal = jnp.sum(jnp.where(row == lane, left, 0.0), axis=1, keepdims=True)
+    return right * lax.rsqrt(diagonal)
+
+
+def kernel(
+    grad_q, error_q, grad_o, error_o, start_q, start_o, weight_q, weight_o, moment_q, moment_o,
+    grad_v, moment_v, weight_v,
+    new_error_q, new_error_o, new_moment_q, new_moment_o, new_weight_q, new_weight_o, new_moment_v, new_weight_v,
+    tot, yrecv, zrecv, blk, wall, xq, xo, scat, got, gath, pall, fall, vpart, vrecv, vall,
+    send_sem, recv_sem,
+):
+    s, t = lax.axis_index("shard"), lax.axis_index("tensor")
+    z, y = s // Y, s % Y
+    barrier = pltpu.get_barrier_semaphore()
+    for k in range(1, SHARD):
+        pl.semaphore_signal(barrier, inc=1, device_id=((s + k) % SHARD, t), device_id_type=pl.DeviceIdType.MESH)
+    for k in range(1, TENSOR):
+        pl.semaphore_signal(barrier, inc=1, device_id=(s, (t + k) % TENSOR), device_id_type=pl.DeviceIdType.MESH)
+
+    used = [0]
+    sent = []
+
+    def copy(src, dst, device):
+        slot = used[0]
+        used[0] += 1
+        out = pltpu.make_async_remote_copy(
+            src_ref=src, dst_ref=dst, send_sem=send_sem.at[slot], recv_sem=recv_sem.at[slot],
+            device_id=device, device_id_type=pl.DeviceIdType.MESH)
+        out.start()
+        sent.append(out)
+        return slot
+
+    def arrived(slot, buffer):
+        pltpu.make_async_remote_copy(
+            src_ref=buffer, dst_ref=buffer, send_sem=send_sem.at[slot], recv_sem=recv_sem.at[slot],
+            device_id=(s, (t + 1) % TENSOR), device_id_type=pl.DeviceIdType.MESH).wait_recv()
+
+    def spread_shard(buf):
+        slots = [copy(buf.at[s], buf.at[s], ((s + k) % SHARD, t)) for k in range(1, SHARD)]
+
+        def wait():
+            for k, slot in enumerate(slots, 1):
+                arrived(slot, buf.at[(s + SHARD - k) % SHARD])
+        return wait
+
+    def spread_tensor(buf):
+        slots = [copy(buf.at[t], buf.at[t], (s, (t + k) % TENSOR)) for k in range(1, TENSOR)]
+
+        def wait():
+            for k, slot in enumerate(slots, 1):
+                arrived(slot, buf.at[(t + TENSOR - k) % TENSOR])
+        return wait
+
+    def scatter_shard(src, dst):
+        slots = [copy(src.at[(s + k) % SHARD], dst.at[k - 1], ((s + k) % SHARD, t)) for k in range(1, SHARD)]
+
+        def wait():
+            for k, slot in enumerate(slots, 1):
+                arrived(slot, dst.at[k - 1])
+        return wait
+
+    for j in range(SHARD):
+        tot[j, 0] = grad_q[j * B : (j + 1) * B, :].astype(f32) + error_q[j * B : (j + 1) * B, :]
+        tot[j, 1] = grad_o[:, j * B : (j + 1) * B].astype(f32) + error_o[:, j * B : (j + 1) * B]
+    pl.semaphore_wait(barrier, SHARD - 1 + TENSOR - 1)
+
+    partner = (z * Y + 1 - y, t)
+    order = [(z + k) % Z for k in (1, 2, 3, 0)]
+    y_slots = [copy(tot.at[c * Y + 1 - y], yrecv.at[c], partner) for c in order]
+    wall[s, 0] = weight_q[...] - 0.01 * (0.9 * moment_q[...])
+    wall[s, 1] = weight_o[...] - 0.01 * (0.9 * moment_o[...])
+    vec = grad_v[...].astype(f32)
+    length = moment_v.shape[1]
+    vpart[...] = jnp.zeros_like(vpart)
+    vall[s] = jnp.zeros((1, VEC_PAD), f32)
+    for j in range(SHARD):
+        vpart[j, :, 0:length] = vec[:, j * length : (j + 1) * length]
+    vector_wait = scatter_shard(vpart, vrecv)
+    z_slots = []
+    for c, slot in zip(order[:3], y_slots[:3]):
+        arrived(slot, yrecv.at[c])
+        yrecv[c] = yrecv[c] + tot[c * Y + y]
+        z_slots.append(copy(yrecv.at[c], zrecv.at[len(z_slots)], (c * Y + y, t)))
+    arrived(y_slots[3], yrecv.at[z])
+    total = yrecv[z] + tot[s]
+    w_slots = [copy(wall.at[s], wall.at[s], (((z + k) % Z) * Y + y, t)) for k in (1, 2, 3)]
+    w_y_slots = [copy(wall.at[s], wall.at[s], partner)]
+
+    def forward(k):
+        c = ((z + Z - k) % Z) * Y + y
+        arrived(w_slots[k - 1], wall.at[c])
+        w_y_slots.append(copy(wall.at[c], wall.at[c], partner))
+
+    for k, slot in enumerate(z_slots):
+        arrived(slot, zrecv.at[k])
+        total = total + zrecv[k]
+    blk[...] = total
+
+    vector_wait()
+    vector_sum = vpart[s]
+    for k in range(SHARD - 1):
+        vector_sum = vector_sum + vrecv[k]
+    moment = 0.9 * moment_v[...] + vector_sum[:, 0:length] / SHARD
+    new_moment_v[...] = moment
+    vall[s, :, 0:length] = weight_v[...] - 0.01 * moment
+    vall_wait = spread_shard(vall)
+
+    factor_q = start_q[...].T
+    factor_o = start_o[pl.ds(pl.multiple_of(s * B, B), B), :].T
+    inverse_q = inverse_o = None
+    for turn in range(ROUNDS):
+        last = turn == ROUNDS - 1
+        a, b = 2 * turn, 2 * turn + 1
+        part_o = nt(factor_o, blk[1])
+        for j in range(RANK // 8):
+            scat[a, j] = part_o[8 * j : 8 * j + 8]
+            scat[a, j + RANK // 8] = jnp.zeros((8, B), f32)
+        scat_wait = scatter_shard(scat.at[a], got.at[a])
+        xq[turn, t] = nt(factor_q, blk[0])
+        xq_wait = spread_tensor(xq.at[turn])
+        if turn:
+            inverse_q, inverse_o = inverse_lower(gram_q), inverse_lower(gram_o)
+        xq_wait()
+        left_q = xq[turn, 0] + xq[turn, 1] + xq[turn, 2] + xq[turn, 3]
+        if turn:
+            left_q = nn(inverse_q, left_q)
+        right_q = nn(left_q, blk[0])
+        square_q = nt(left_q, left_q)
+        for j in range(RANK // 8):
+            scat[b, j] = right_q[8 * j : 8 * j + 8]
+            scat[b, j + RANK // 8] = jnp.zeros((8, B), f32)
+            scat[b, j + RANK // 8, :, 0:RANK] = square_q[8 * j : 8 * j + 8]
+        q_wait = scatter_shard(scat.at[b], got.at[b])
+        scat_wait()
+        piece = scat[a, s]
+        for k in range(SHARD - 1):
+            piece = piece + got[a, k]
+        gath[a, s] = piece
+        o_wait = spread_shard(gath.at[a])
+        if last:
+            pall[s] = left_q
+            pall_wait = spread_shard(pall)
+            forward(1)
+        q_wait()
+        piece = scat[b, s]
+        for k in range(SHARD - 1):
+            piece = piece + got[b, k]
+        gath[b, s] = piece
+        q_wait = spread_shard(gath.at[b])
+        o_wait()
+        left_o = gath[a, 0 : RANK // 8].reshape(RANK, B)
+        if turn:
+            left_o = nn(inverse_o, left_o)
+        xo[turn, t, 0:RANK] = nn(left_o, blk[1])
+        xo[turn, t, RANK : 2 * RANK] = jnp.zeros((RANK, B), f32)
+        xo[turn, t, RANK : 2 * RANK, 0:RANK] = nt(left_o, left_o)
+        xo_wait = spread_tensor(xo.at[turn])
+        if last:
+            forward(2)
+        q_wait()
+        factor_q = gath[b, 0 : RANK // 8].reshape(RANK, B)
+        gram_q = gath[b, RANK // 8 : SHARD].reshape(RANK, B)[:, 0:RANK]
+        xo_wait()
+        both = xo[turn, 0] + xo[turn, 1] + xo[turn, 2] + xo[turn, 3]
+        factor_o, gram_o = both[0:RANK], both[RANK : 2 * RANK, 0:RANK]
+
+    fall[s] = factor_o
+    fall_wait = spread_shard(fall)
+    forward(3)
+    inverse_q, inverse_o = inverse_lower(gram_q), inverse_lower(gram_o)
+    side_q = nn(inverse_q.T, nn(inverse_q, factor_q)) / SHARD
+    side_o = (nn(inverse_o.T, nn(inverse_o, left_o)) / SHARD).T
+    new_moment_q[...] = 0.9 * moment_q[...] + nn(left_q.T, side_q)
+    new_moment_o[...] = 0.9 * moment_o[...] + nn(side_o, factor_o)
+    pall_wait()
+    own = [(z + Z - k) % Z for k in (0, 1, 2, 3)]
+    for c, slot in zip(own, w_y_slots):
+        arrived(slot, wall.at[c * Y + 1 - y])
+    for j in range(SHARD):
+        approx = nn(pall[j].T, side_q)
+        new_error_q[j * B : (j + 1) * B, :] = tot[j, 0] - approx
+        new_weight_q[j * B : (j + 1) * B, :] = wall[j, 0] - 0.01 * approx
+    fall_wait()
+    for j in range(SHARD):
+        approx = nn(side_o, fall[j])
+        new_error_o[:, j * B : (j + 1) * B] = tot[j, 1] - approx
+        new_weight_o[:, j * B : (j + 1) * B] = wall[j, 1] - 0.01 * approx
+    vall_wait()
+    new_weight_v[...] = vall[...]
+    for out in sent:
+        out.wait_send()
+
+
+def fast_local(
+    grad_query, error_query, grad_output, error_output, start_query, start_output, weight_query, weight_output,
+    moment_query, moment_output, grad_vector, moment_vector, weight_vector,
+):
+    length = moment_vector.shape[0]
+    vmem = pl.BlockSpec(memory_space=pltpu.VMEM)
+    shape = lambda *dims: jax.ShapeDtypeStruct(dims, f32)
+    scratch = lambda *dims: pltpu.VMEM(dims, f32)
+    eq, eo, mq, mo, wq, wo, mv, wv = pl.pallas_call(
+        kernel,
+        out_shape=(
+            shape(SHARD * B, B), shape(B, SHARD * B), shape(B, B), shape(B, B),
+            shape(SHARD * B, B), shape(B, SHARD * B), shape(1, length), shape(SHARD, 1, VEC_PAD),
+        ),
+        in_specs=[vmem] * 13,
+        out_specs=(vmem,) * 8,
+        scratch_shapes=[
+            scratch(SHARD, 2, B, B), scratch(Z, 2, B, B), scratch(Z - 1, 2, B, B), scratch(2, B, B),
+            scratch(SHARD, 2, B, B), scratch(ROUNDS, TENSOR, RANK, B), scratch(ROUNDS, TENSOR, 2 * RANK, B),
+            scratch(2 * ROUNDS, SHARD, 8, B), scratch(2 * ROUNDS, SHARD - 1, 8, B), scratch(2 * ROUNDS, SHARD, 8, B),
+            scratch(SHARD, RANK, B), scratch(SHARD, RANK, B),
+            scratch(SHARD, 1, VEC_PAD), scratch(SHARD - 1, 1, VEC_PAD), scratch(SHARD, 1, VEC_PAD),
+            pltpu.SemaphoreType.DMA((SLOTS,)), pltpu.SemaphoreType.DMA((SLOTS,)),
+        ],
+        compiler_params=pltpu.CompilerParams(collective_id=0, has_side_effects=True, vmem_limit_bytes=40 * 2**20),
+        cost_estimate=pl.CostEstimate(flops=2**30, bytes_accessed=5 * 2**20, transcendentals=0),
+    )(
+        grad_query[0], error_query[0], grad_output[0], error_output[0], start_query, start_output,
+        weight_query, weight_output, moment_query, moment_output,
+        grad_vector, moment_vector[None], weight_vector[None],
+    )
+    return eq[None], eo[None], mq, mo, wq, wo, mv[0], wv[:, 0, 0:length].reshape(-1)
+
+
 def solution(mesh):
     in_specs = (
         P("shard", None, "tensor"),
@@ -129,4 +383,5 @@
         P("shard"),
         P(),
     )
-    return jax.shard_map(local, mesh=mesh, in_specs=in_specs, out_specs=out_specs, check_vma=False)
+    body = fast_local if (mesh.shape["shard"], mesh.shape["tensor"]) == (Z * Y, TENSOR) else local
+    return jax.shard_map(body, mesh=mesh, in_specs=in_specs, out_specs=out_specs, check_vma=False)

time: 513 us -> 83.3 us (0.16)
  waiting for transfers between devices: 249 us -> 0 us
  blocking collectives: 197 us -> 0 us
  Pallas kernels: 0 us -> 69.9 us
  other arithmetic: 30.5 us -> 0 us
  matrix products: 16.5 us -> 0 us
  between operations: 15 us -> 0.77 us
  local copies, waits for them, and re-layouts: 4.7 us -> 12.3 us
    psum x2 -> x0, waiting for transfers between devices: 249 us -> none  [local(): sum_query = lax.psum(part_query, ('shard', 'tensor'))]
    psum x5 -> x0, blocking collectives: 134 us -> none  [the longest x2 74.6 us: local(): factor_query = lax.psum(right_query_part, 'shard')]
    pallas_call x0 -> x1, Pallas kernels: none -> 69.9 us  [fast_local(): pl.pallas_call(kernel, out_shape=(shape(SHARD * B, B), shape(B, SHARD * B...]
    all_gather x2 -> x0, blocking collectives: 63 us -> none  [the longest x1 31.8 us: local(): lax.all_gather(stepped_query, 'shard', axis=0, tiled=True)]
    another operation x20 -> x0, other arithmetic: 26.8 us -> none  [the longest x12 14.4 us: solve_rows(): lower = jnp.linalg.cholesky(gram)]
    dot_general x14 -> x0, matrix products: 15.4 us -> none  [the longest x6 9.08 us: product(): jnp.dot(left, right, precision=highest, preferred_element_type=jnp.float32)]
    unnamed x36 -> x31, local copies, waits for them, and re-layouts: 4.41 us -> 11.5 us
  transfers between devices with their start and end apart: 2 -> 0, of which waited for: 2 -> 0; matrix products, arithmetic and copies ran while one was open for 0% -> 0% of each run, Pallas kernels for 0% -> 0%
where the time goes in v1:
time: 83.3 us; the launch traced here: 83 us
  Pallas kernels  69.9 us (84%)
  local copies, waits for them, and re-layouts  12.3 us (15%)
    pallas_call x1, Pallas kernels, fast_local(): pl.pallas_call(kernel, out_shape=(shape(SHARD * B, B), shape(B, SHARD * B...  69.9 us
    unnamed x31, local copies, waits for them, and re-layouts  11.5 us

profile of v1, /device:TPU:0, one launch (start us, length us, event | category | flops | bytes accessed | tf_op | source)
XLA Modules:
  0.0 83.0 jit_solution(2437340425124940734)
XLA Ops:
  0.6 0.0 copy-start
  0.6 0.9 %copy.21.start_q = f32[128,32]{1,0:T(8,128)S(1)} copy(f32[128,32]{0,1:T(8,128)} %param.17) | data formatting | bytes 32768 | tf_op args[4]
  1.5 0.0 copy-start.4
  1.5 0.0 copy-start.5
  1.5 0.0 copy-start.6
  1.5 0.0 copy-start.9
  1.6 0.0 copy-start.10
  1.6 1.1 %copy.22.start_o = f32[1024,32]{1,0:T(8,128)S(1)} copy(f32[1024,32]{0,1:T(8,128)} %param.18) | data formatting | bytes 262144 | tf_op args[5]
  2.7 0.0 copy-done
  2.8 0.0 copy-start.1
  2.8 1.0 %copy-done.1 = f32[1,128,1024]{2,1,0:T(8,128)S(1)} copy-done((f32[1,128,1024]{2,1,0:T(8,128)S(1)}, f32[1,128,1024]{2,1,0:T(8,128)}, u32[]{:S(2)}) %copy-start.1) | copy-done | bytes 524312
  3.8 0.9 %copy-done.2 = bf16[1,1024,128]{2,1,0:T(8,128)(2,1)S(1)} copy-done((bf16[1,1024,128]{2,1,0:T(8,128)(2,1)S(1)}, bf16[1,1024,128]{2,1,0:T(8,128)(2,1)}, u32[]{:S(2)}) %copy-start.2) | copy-done | bytes 262168
  4.8 0.9 %copy-done.3 = bf16[1,128,1024]{2,1,0:T(8,128)(2,1)S(1)} copy-done((bf16[1,128,1024]{2,1,0:T(8,128)(2,1)S(1)}, bf16[1,128,1024]{2,1,0:T(8,128)(2,1)}, u32[]{:S(2)}) %copy-start.3) | copy-done | bytes 262168
  5.7 0.8 %copy-done.7 = f32[128,128]{1,0:T(8,128)S(1)} copy-done((f32[128,128]{1,0:T(8,128)S(1)}, f32[128,128]{1,0:T(8,128)}, u32[]{:S(2)}) %copy-start.7) | copy-done | bytes 65560
  6.6 0.7 copy-done.8
  7.3 69.9 %shard_map.188 = (f32[1024,128]{1,0:T(8,128)S(1)}, f32[128,1024]{1,0:T(8,128)S(1)}, f32[128,128]{1,0:T(8,128)S(1)}, f32[128,128]{1,0:T(8,128)S(1)}, f32[1024,128...) custom-call(bf16[1024,128]{1,0:T(8,128)(2,1)S(1)} %bitcast.14, ...), custom_call_target="tpu_custom_call" | custom-call | flops 1073741824 | bytes 5242880 | tf_op jit(solution)/shard_map/pallas_call | solution.py:334
  77.3 0.7 reshape_squeeze.3
  77.9 0.8 copy.30
  78.7 0.8 copy.31
  79.5 0.6 copy.32
  80.2 0.6 copy.33
  80.8 0.8 copy.34
  81.6 0.8 copy.35
  82.4 0.6 copy.36
  (10 shorter events, 0.1 us)
Async XLA Ops:
  0.6 2.1 %copy-start = (f32[1,1024,128]{2,1,0:T(8,128)S(1)}, f32[1,1024,128]{2,1,0:T(8,128)}, u32[]{:S(2)}) copy-start(f32[1,1024,128]{2,1,0:T(8,128)} %param.14) | copy-start | bytes 1572868
  1.5 1.2 %copy-start.4 = (f32[128,128]{1,0:T(8,128)S(1)}, f32[128,128]{1,0:T(8,128)}, u32[]{:S(2)}) copy-start(f32[128,128]{1,0:T(8,128)} %weight_q.1) | copy-start | bytes 196612
  1.5 1.2 %copy-start.5 = (f32[128,128]{1,0:T(8,128)S(1)}, f32[128,128]{1,0:T(8,128)}, u32[]{:S(2)}) copy-start(f32[128,128]{1,0:T(8,128)} %weight_o.1) | copy-start | bytes 196612
  1.5 1.2 %copy-start.6 = (f32[128,128]{1,0:T(8,128)S(1)}, f32[128,128]{1,0:T(8,128)}, u32[]{:S(2)}) copy-start(f32[128,128]{1,0:T(8,128)} %moment_q.1) | copy-start | bytes 196612
  1.5 1.2 %copy-start.9 = (f32[448]{0:T(512)S(1)}, f32[448]{0:T(512)}, u32[]{:S(2)}) copy-start(f32[448]{0:T(512)} %param.24) | copy-start | bytes 5380
  1.6 1.2 %copy-start.10 = (f32[448]{0:T(512)S(1)}, f32[448]{0:T(512)}, u32[]{:S(2)}) copy-start(f32[448]{0:T(512)} %param.25) | copy-start | bytes 5380
  2.8 1.0 %copy-start.1 = (f32[1,128,1024]{2,1,0:T(8,128)S(1)}, f32[1,128,1024]{2,1,0:T(8,128)}, u32[]{:S(2)}) copy-start(f32[1,128,1024]{2,1,0:T(8,128)} %param.16) | copy-start | bytes 1572868
  3.8 0.9 %copy-start.2 = (bf16[1,1024,128]{2,1,0:T(8,128)(2,1)S(1)}, bf16[1,1024,128]{2,1,0:T(8,128)(2,1)}, u32[]{:S(2)}) copy-start(bf16[1,1024,128]{2,1,0:T(8,128)(2,1)} %param.13) | copy-start | bytes 786436
  4.8 0.9 %copy-start.3 = (bf16[1,128,1024]{2,1,0:T(8,128)(2,1)S(1)}, bf16[1,128,1024]{2,1,0:T(8,128)(2,1)}, u32[]{:S(2)}) copy-start(bf16[1,128,1024]{2,1,0:T(8,128)(2,1)} %param.15) | copy-start | bytes 786436
  5.7 0.8 %copy-start.7 = (f32[128,128]{1,0:T(8,128)S(1)}, f32[128,128]{1,0:T(8,128)}, u32[]{:S(2)}) copy-start(f32[128,128]{1,0:T(8,128)} %moment_o.1) | copy-start | bytes 196612
  6.6 0.7 copy-start.8

commit v2 on v1

--- a/solution.py
+++ b/solution.py
@@ -110,7 +110,7 @@
 RANK = 32
 B = 128
 VEC_PAD = 512
-SLOTS = 128
+SLOTS = 40
 f32 = jnp.float32
 
 
@@ -126,10 +126,21 @@
     row = lax.broadcasted_iota(jnp.int32, (RANK, RANK), 0)
     lane = lax.broadcasted_iota(jnp.int32, (RANK, RANK), 1)
     left, right = gram, (row == lane).astype(f32)
-    row_of = lax.broadcasted_iota(jnp.int32, (RANK, 1), 0)
-    for k in range(RANK):
-        ratio = jnp.where(row_of > k, left[:, k : k + 1] * (1.0 / left[k : k + 1, k : k + 1]), 0.0)
-        left, right = left - ratio * left[k : k + 1, :], right - ratio * right[k : k + 1, :]
+    for k in range(0, RANK, 2):
+        first = jnp.broadcast_to(left[:, k : k + 1], (RANK, RANK))
+        second = jnp.broadcast_to(left[:, k + 1 : k + 2], (RANK, RANK))
+        over = 1.0 / first[k : k + 1]
+        cross = first[k + 1 : k + 2]
+        ratio = cross * over
+        under = 1.0 / (second[k + 1 : k + 2] - cross * ratio)
+
+        def reduced(matrix):
+            top, low = matrix[k : k + 1], matrix[k + 1 : k + 2]
+            low = (low - ratio * matrix[k : k + 1]) * under
+            rest = first * (top * over - ratio * low) + second * low
+            return matrix - jnp.where(row > k + 1, rest, jnp.where(row == k + 1, ratio * top, 0.0))
+
+        left, right = reduced(left), reduced(right)
     diagonal = jnp.sum(jnp.where(row == lane, left, 0.0), axis=1, keepdims=True)
     return right * lax.rsqrt(diagonal)
 
@@ -137,70 +148,68 @@
 def kernel(
     grad_q, error_q, grad_o, error_o, start_q, start_o, weight_q, weight_o, moment_q, moment_o,
     grad_v, moment_v, weight_v,
-    new_error_q, new_error_o, new_moment_q, new_moment_o, new_weight_q, new_weight_o, new_moment_v, new_weight_v,
-    tot, yrecv, zrecv, blk, wall, xq, xo, scat, got, gath, pall, fall, vpart, vrecv, vall,
-    send_sem, recv_sem,
+    keep_tot, keep_wall, keep_pall, keep_fall, keep_q, keep_o, keep_moments, keep_vall, new_moment_v,
+    tot, wall, pall, fall, side_q, side_o, moments, vall, gq, eq, go, eo, sq, so, weights, yrecv, zrecv, blk, xq, xo, scat, got, gath, vpart, vrecv,
+    send_sem, recv_sem, load_sem, keep_sem,
 ):
     s, t = lax.axis_index("shard"), lax.axis_index("tensor")
     z, y = s // Y, s % Y
+    loads = [pltpu.make_async_copy(src, dst, load_sem.at[i])
+             for i, (src, dst) in enumerate((
+                 (grad_q, gq), (error_q, eq), (grad_o, go), (error_o, eo), (start_q, sq), (start_o, so),
+                 (weight_q, weights.at[0]), (weight_o, weights.at[1]),
+                 (moment_q, moments.at[0]), (moment_o, moments.at[1]),
+             ))]
+    for load in loads:
+        load.start()
     barrier = pltpu.get_barrier_semaphore()
     for k in range(1, SHARD):
         pl.semaphore_signal(barrier, inc=1, device_id=((s + k) % SHARD, t), device_id_type=pl.DeviceIdType.MESH)
     for k in range(1, TENSOR):
         pl.semaphore_signal(barrier, inc=1, device_id=(s, (t + k) % TENSOR), device_id_type=pl.DeviceIdType.MESH)
 
+    kept = []
+
+    def keep(src, dst):
+        copy = pltpu.make_async_copy(src, dst, keep_sem.at[len(kept)])
+        copy.start()
+        kept.append(copy)
+
     used = [0]
     sent = []
 
-    def copy(src, dst, device):
+    def group(copies, many):
         slot = used[0]
         used[0] += 1
-        out = pltpu.make_async_remote_copy(
-            src_ref=src, dst_ref=dst, send_sem=send_sem.at[slot], recv_sem=recv_sem.at[slot],
-            device_id=device, device_id_type=pl.DeviceIdType.MESH)
-        out.start()
-        sent.append(out)
-        return slot
-
-    def arrived(slot, buffer):
-        pltpu.make_async_remote_copy(
-            src_ref=buffer, dst_ref=buffer, send_sem=send_sem.at[slot], recv_sem=recv_sem.at[slot],
-            device_id=(s, (t + 1) % TENSOR), device_id_type=pl.DeviceIdType.MESH).wait_recv()
+        for src, dst, device in copies:
+            pltpu.make_async_remote_copy(
+                src_ref=src, dst_ref=dst, send_sem=send_sem.at[slot], recv_sem=recv_sem.at[slot],
+                device_id=device, device_id_type=pl.DeviceIdType.MESH).start()
+        sent.append((many, slot))
+        return lambda: pltpu.make_async_copy(many, many, recv_sem.at[slot]).wait()
 
     def spread_shard(buf):
-        slots = [copy(buf.at[s], buf.at[s], ((s + k) % SHARD, t)) for k in range(1, SHARD)]
-
-        def wait():
-            for k, slot in enumerate(slots, 1):
-                arrived(slot, buf.at[(s + SHARD - k) % SHARD])
-        return wait
+        return group([(buf.at[s], buf.at[s], ((s + k) % SHARD, t)) for k in range(1, SHARD)], buf.at[pl.ds(0, SHARD - 1)])
 
     def spread_tensor(buf):
-        slots = [copy(buf.at[t], buf.at[t], (s, (t + k) % TENSOR)) for k in range(1, TENSOR)]
-
-        def wait():
-            for k, slot in enumerate(slots, 1):
-                arrived(slot, buf.at[(t + TENSOR - k) % TENSOR])
-        return wait
+        return group([(buf.at[t], buf.at[t], (s, (t + k) % TENSOR)) for k in range(1, TENSOR)], buf.at[pl.ds(0, TENSOR - 1)])
 
     def scatter_shard(src, dst):
-        slots = [copy(src.at[(s + k) % SHARD], dst.at[k - 1], ((s + k) % SHARD, t)) for k in range(1, SHARD)]
-
-        def wait():
-            for k, slot in enumerate(slots, 1):
-                arrived(slot, dst.at[k - 1])
-        return wait
-
+        return group([(src.at[(s + k) % SHARD], dst.at[k - 1], ((s + k) % SHARD, t)) for k in range(1, SHARD)], dst)
+
+    for load in loads:
+        load.wait()
     for j in range(SHARD):
-        tot[j, 0] = grad_q[j * B : (j + 1) * B, :].astype(f32) + error_q[j * B : (j + 1) * B, :]
-        tot[j, 1] = grad_o[:, j * B : (j + 1) * B].astype(f32) + error_o[:, j * B : (j + 1) * B]
+        tot[j, 0] = gq[j * B : (j + 1) * B, :].astype(f32) + eq[j * B : (j + 1) * B, :]
+        tot[j, 1] = go[:, j * B : (j + 1) * B].astype(f32) + eo[:, j * B : (j + 1) * B]
     pl.semaphore_wait(barrier, SHARD - 1 + TENSOR - 1)
 
     partner = (z * Y + 1 - y, t)
     order = [(z + k) % Z for k in (1, 2, 3, 0)]
-    y_slots = [copy(tot.at[c * Y + 1 - y], yrecv.at[c], partner) for c in order]
-    wall[s, 0] = weight_q[...] - 0.01 * (0.9 * moment_q[...])
-    wall[s, 1] = weight_o[...] - 0.01 * (0.9 * moment_o[...])
+    y_waits = [group([(tot.at[c * Y + 1 - y], yrecv.at[c], partner)], yrecv.at[c]) for c in order]
+    keep(tot, keep_tot)
+    keep(moments, keep_moments)
+    wall[s] = weights[...] - 0.01 * (0.9 * moments[...])
     vec = grad_v[...].astype(f32)
     length = moment_v.shape[1]
     vpart[...] = jnp.zeros_like(vpart)
@@ -208,23 +217,23 @@
     for j in range(SHARD):
         vpart[j, :, 0:length] = vec[:, j * length : (j + 1) * length]
     vector_wait = scatter_shard(vpart, vrecv)
-    z_slots = []
-    for c, slot in zip(order[:3], y_slots[:3]):
-        arrived(slot, yrecv.at[c])
+    z_waits = []
+    for k, c in enumerate(order[:3]):
+        y_waits[k]()
         yrecv[c] = yrecv[c] + tot[c * Y + y]
-        z_slots.append(copy(yrecv.at[c], zrecv.at[len(z_slots)], (c * Y + y, t)))
-    arrived(y_slots[3], yrecv.at[z])
+        z_waits.append(group([(yrecv.at[c], zrecv.at[k], (c * Y + y, t))], zrecv.at[k]))
+    y_waits[3]()
     total = yrecv[z] + tot[s]
-    w_slots = [copy(wall.at[s], wall.at[s], (((z + k) % Z) * Y + y, t)) for k in (1, 2, 3)]
-    w_y_slots = [copy(wall.at[s], wall.at[s], partner)]
+    w_waits = [group([(wall.at[s], wall.at[s], (((z + k) % Z) * Y + y, t))], wall.at[((z + Z - k) % Z) * Y + y]) for k in (1, 2, 3)]
+    w_y_waits = [group([(wall.at[s], wall.at[s], partner)], wall.at[z * Y + 1 - y])]
 
     def forward(k):
-        c = ((z + Z - k) % Z) * Y + y
-        arrived(w_slots[k - 1], wall.at[c])
-        w_y_slots.append(copy(wall.at[c], wall.at[c], partner))
-
-    for k, slot in enumerate(z_slots):
-        arrived(slot, zrecv.at[k])
+        c = (z + Z - k) % Z
+        w_waits[k - 1]()
+        w_y_waits.append(group([(wall.at[c * Y + y], wall.at[c * Y + y], partner)], wall.at[c * Y + 1 - y]))
+
+    for k in range(Z - 1):
+        z_waits[k]()
         total = total + zrecv[k]
     blk[...] = total
 
@@ -237,8 +246,8 @@
     vall[s, :, 0:length] = weight_v[...] - 0.01 * moment
     vall_wait = spread_shard(vall)
 
-    factor_q = start_q[...].T
-    factor_o = start_o[pl.ds(pl.multiple_of(s * B, B), B), :].T
+    factor_q = sq[...]
+    factor_o = so[:, pl.ds(pl.multiple_of(s * B, B), B)]
     inverse_q = inverse_o = None
     for turn in range(ROUNDS):
         last = turn == ROUNDS - 1
@@ -272,7 +281,7 @@
         if last:
             pall[s] = left_q
             pall_wait = spread_shard(pall)
-            forward(1)
+            forward(2)
         q_wait()
         piece = scat[b, s]
         for k in range(SHARD - 1):
@@ -287,8 +296,7 @@
         xo[turn, t, RANK : 2 * RANK] = jnp.zeros((RANK, B), f32)
         xo[turn, t, RANK : 2 * RANK, 0:RANK] = nt(left_o, left_o)
         xo_wait = spread_tensor(xo.at[turn])
-        if last:
-            forward(2)
+        forward(3 if last else 1)
         q_wait()
         factor_q = gath[b, 0 : RANK // 8].reshape(RANK, B)
         gram_q = gath[b, RANK // 8 : SHARD].reshape(RANK, B)[:, 0:RANK]
@@ -298,29 +306,72 @@
 
     fall[s] = factor_o
     fall_wait = spread_shard(fall)
-    forward(3)
     inverse_q, inverse_o = inverse_lower(gram_q), inverse_lower(gram_o)
-    side_q = nn(inverse_q.T, nn(inverse_q, factor_q)) / SHARD
-    side_o = (nn(inverse_o.T, nn(inverse_o, left_o)) / SHARD).T
-    new_moment_q[...] = 0.9 * moment_q[...] + nn(left_q.T, side_q)
-    new_moment_o[...] = 0.9 * moment_o[...] + nn(side_o, factor_o)
+    side_q[...] = nn(inverse_q.T, nn(inverse_q, factor_q)) / SHARD
+    side_o[...] = (nn(inverse_o.T, nn(inverse_o, left_o)) / SHARD).T
+    keep(side_q, keep_q)
+    keep(side_o, keep_o)
     pall_wait()
-    own = [(z + Z - k) % Z for k in (0, 1, 2, 3)]
-    for c, slot in zip(own, w_y_slots):
-        arrived(slot, wall.at[c * Y + 1 - y])
+    keep(pall, keep_pall)
+    vall_wait()
+    keep(vall, keep_vall)
+    fall_wait()
+    keep(fall, keep_fall)
+    for wait in w_y_waits:
+        wait()
+    keep(wall, keep_wall)
+    for many, slot in sent:
+        pltpu.make_async_copy(many, many, send_sem.at[slot]).wait()
+    for copy in kept:
+        copy.wait()
+
+
+def finish(
+    keep_tot, keep_wall, keep_pall, keep_fall, keep_q, keep_o, keep_moments, keep_vall, moment_v,
+    new_error_q, new_error_o, new_moment_q, new_moment_o, new_weight_q, new_weight_o, new_moment_v, new_weight_v,
+    tot, wall, pall, fall, side_q, side_o, moments, vall, eq, eo, mq, mo, wq, wo, sem, load_sem,
+):
+    pairs = (
+        (keep_q, side_q), (keep_o, side_o), (keep_pall, pall), (keep_fall, fall), (keep_moments, moments),
+        (keep_tot, tot), (keep_wall, wall), (keep_vall, vall),
+    )
+    loads = [pltpu.make_async_copy(src, dst, load_sem.at[i]) for i, (src, dst) in enumerate(pairs)]
+    for load in loads:
+        load.start()
+    s = lax.axis_index("shard")
+    out = []
+
+    def leave(src, dst):
+        copy = pltpu.make_async_copy(src, dst, sem.at[len(out)])
+        copy.start()
+        out.append(copy)
+
+    for load in loads:
+        load.wait()
+    mq[...] = 0.9 * moments[0] + nn(pall[s].T, side_q[...])
+    mo[...] = 0.9 * moments[1] + nn(side_o[...], fall[s])
+    leave(mq, new_moment_q)
+    leave(mo, new_moment_o)
     for j in range(SHARD):
-        approx = nn(pall[j].T, side_q)
-        new_error_q[j * B : (j + 1) * B, :] = tot[j, 0] - approx
-        new_weight_q[j * B : (j + 1) * B, :] = wall[j, 0] - 0.01 * approx
-    fall_wait()
+        rows = pl.ds(j * B, B)
+        approx = nn(pall[j].T, side_q[...])
+        eq[rows, :] = tot[j, 0] - approx
+        wq[rows, :] = wall[j, 0] - 0.01 * approx
+        approx = nn(side_o[...], fall[j])
+        eo[:, rows] = tot[j, 1] - approx
+        wo[:, rows] = wall[j, 1] - 0.01 * approx
+        if j % 2:
+            pair = pl.ds((j - 1) * B, 2 * B)
+            leave(eq.at[pair, :], new_error_q.at[pair, :])
+            leave(wq.at[pair, :], new_weight_q.at[pair, :])
+            leave(eo.at[:, pair], new_error_o.at[:, pair])
+            leave(wo.at[:, pair], new_weight_o.at[:, pair])
+    length = moment_v.shape[1]
+    new_moment_v[...] = moment_v[...]
     for j in range(SHARD):
-        approx = nn(side_o, fall[j])
-        new_error_o[:, j * B : (j + 1) * B] = tot[j, 1] - approx
-        new_weight_o[:, j * B : (j + 1) * B] = wall[j, 1] - 0.01 * approx
-    vall_wait()
-    new_weight_v[...] = vall[...]
-    for out in sent:
-        out.wait_send()
+        new_weight_v[:, j * length : (j + 1) * length] = vall[j, :, 0:length]
+    for copy in out:
+        copy.wait()
 
 
 def fast_local(
@@ -329,32 +380,55 @@
 ):
     length = moment_vector.shape[0]
     vmem = pl.BlockSpec(memory_space=pltpu.VMEM)
+    hbm = pl.BlockSpec(memory_space=pltpu.HBM)
     shape = lambda *dims: jax.ShapeDtypeStruct(dims, f32)
     scratch = lambda *dims: pltpu.VMEM(dims, f32)
-    eq, eo, mq, mo, wq, wo, mv, wv = pl.pallas_call(
+    kept = pl.pallas_call(
         kernel,
         out_shape=(
-            shape(SHARD * B, B), shape(B, SHARD * B), shape(B, B), shape(B, B),
-            shape(SHARD * B, B), shape(B, SHARD * B), shape(1, length), shape(SHARD, 1, VEC_PAD),
+            shape(SHARD, 2, B, B), shape(SHARD, 2, B, B), shape(SHARD, RANK, B), shape(SHARD, RANK, B),
+            shape(RANK, B), shape(B, RANK), shape(2, B, B), shape(SHARD, 1, VEC_PAD), shape(1, length),
         ),
-        in_specs=[vmem] * 13,
-        out_specs=(vmem,) * 8,
+        in_specs=[hbm] * 10 + [vmem] * 3,
+        out_specs=(hbm,) * 8 + (vmem,),
         scratch_shapes=[
-            scratch(SHARD, 2, B, B), scratch(Z, 2, B, B), scratch(Z - 1, 2, B, B), scratch(2, B, B),
-            scratch(SHARD, 2, B, B), scratch(ROUNDS, TENSOR, RANK, B), scratch(ROUNDS, TENSOR, 2 * RANK, B),
+            scratch(SHARD, 2, B, B), scratch(SHARD, 2, B, B), scratch(SHARD, RANK, B), scratch(SHARD, RANK, B),
+            scratch(RANK, B), scratch(B, RANK), scratch(2, B, B), scratch(SHARD, 1, VEC_PAD),
+            pltpu.VMEM((SHARD * B, B), grad_query.dtype), scratch(SHARD * B, B),
+            pltpu.VMEM((B, SHARD * B), grad_output.dtype), scratch(B, SHARD * B),
+            scratch(RANK, B), scratch(RANK, SHARD * B), scratch(2, B, B),
+            scratch(Z, 2, B, B), scratch(Z - 1, 2, B, B), scratch(2, B, B),
+            scratch(ROUNDS, TENSOR, RANK, B), scratch(ROUNDS, TENSOR, 2 * RANK, B),
             scratch(2 * ROUNDS, SHARD, 8, B), scratch(2 * ROUNDS, SHARD - 1, 8, B), scratch(2 * ROUNDS, SHARD, 8, B),
-            scratch(SHARD, RANK, B), scratch(SHARD, RANK, B),
-            scratch(SHARD, 1, VEC_PAD), scratch(SHARD - 1, 1, VEC_PAD), scratch(SHARD, 1, VEC_PAD),
-            pltpu.SemaphoreType.DMA((SLOTS,)), pltpu.SemaphoreType.DMA((SLOTS,)),
+            scratch(SHARD, 1, VEC_PAD), scratch(SHARD - 1, 1, VEC_PAD),
+            pltpu.SemaphoreType.DMA((SLOTS,)), pltpu.SemaphoreType.DMA((SLOTS,)), pltpu.SemaphoreType.DMA((10,)), pltpu.SemaphoreType.DMA((8,)),
         ],
-        compiler_params=pltpu.CompilerParams(collective_id=0, has_side_effects=True, vmem_limit_bytes=40 * 2**20),
+        compiler_params=pltpu.CompilerParams(collective_id=0, has_side_effects=True, vmem_limit_bytes=60 * 2**20),
         cost_estimate=pl.CostEstimate(flops=2**30, bytes_accessed=5 * 2**20, transcendentals=0),
     )(
-        grad_query[0], error_query[0], grad_output[0], error_output[0], start_query, start_output,
+        grad_query[0], error_query[0], grad_output[0], error_output[0], start_query.T, start_output.T,
         weight_query, weight_output, moment_query, moment_output,
         grad_vector, moment_vector[None], weight_vector[None],
     )
-    return eq[None], eo[None], mq, mo, wq, wo, mv[0], wv[:, 0, 0:length].reshape(-1)
+    eq, eo, mq, mo, wq, wo, mv, wv = pl.pallas_call(
+        finish,
+        out_shape=(
+            shape(SHARD * B, B), shape(B, SHARD * B), shape(B, B), shape(B, B),
+            shape(SHARD * B, B), shape(B, SHARD * B), shape(1, length), shape(1, SHARD * length),
+        ),
+        in_specs=[hbm] * 8 + [vmem],
+        out_specs=(hbm,) * 6 + (vmem,) * 2,
+        scratch_shapes=[
+            scratch(SHARD, 2, B, B), scratch(SHARD, 2, B, B), scratch(SHARD, RANK, B), scratch(SHARD, RANK, B),
+            scratch(RANK, B), scratch(B, RANK), scratch(2, B, B), scratch(SHARD, 1, VEC_PAD),
+            scratch(SHARD * B, B), scratch(B, SHARD * B), scratch(B, B), scratch(B, B),
+            scratch(SHARD * B, B), scratch(B, SHARD * B), pltpu.SemaphoreType.DMA((2 + 2 * SHARD,)),
+            pltpu.SemaphoreType.DMA((8,)),
+        ],
+        compiler_params=pltpu.CompilerParams(vmem_limit_bytes=60 * 2**20),
+        cost_estimate=pl.CostEstimate(flops=2**26, bytes_accessed=5 * 2**20, transcendentals=0),
+    )(*kept)
+    return eq[None], eo[None], mq, mo, wq, wo, mv[0], wv[0]
 
 
 def solution(mesh):

time: 83.3 us -> 74.4 us (0.89)
  local copies, waits for them, and re-layouts: 12.3 us -> 0.71 us
  Pallas kernels: 69.9 us -> 72 us
    unnamed x31 -> x2, local copies, waits for them, and re-layouts: 11.5 us -> 0.71 us
    pallas_call x1 -> x2, Pallas kernels: 69.9 us -> 72 us  [the longest x1 66.8 us: fast_local(): pl.pallas_call(kernel, out_shape=(shape(SHARD, 2, B, B), shape(SHARD, 2,...]
where the time goes in v2:
time: 74.4 us; the launch traced here: 74 us
  Pallas kernels  72 us (97%)
    pallas_call x1, Pallas kernels, fast_local(): pl.pallas_call(kernel, out_shape=(shape(SHARD, 2, B, B), shape(SHARD, 2,...  66.8 us
    pallas_call x1, Pallas kernels, fast_local(): pl.pallas_call(finish, out_shape=(shape(SHARD * B, B), shape(B, SHARD * B...  5.24 us

profile of v2, /device:TPU:0, one launch (start us, length us, event | category | flops | bytes accessed | tf_op | source)
XLA Modules:
  0.0 74.0 jit_solution(9678247893535037802)
XLA Ops:
  0.6 66.8 %shard_map.188 = (f32[8,2,128,128]{3,2,1,0:T(8,128)}, f32[8,2,128,128]{3,2,1,0:T(8,128)}, f32[8,32,128]{2,1,0:T(8,128)}, f32[8,32,128]{2,1,0:T(8,128)}, f32[32,1...) custom-call(bf16[1024,128]{1,0:T(8,128)(2,1)} %bitcast.15, ...), custom_call_target="tpu_custom_call" | custom-call | flops 1073741824 | bytes 5242880 | tf_op jit(solution)/shard_map/pallas_call | solution.py:386
  67.4 5.2 %shard_map.189 = (f32[1024,128]{1,0:T(8,128)}, f32[128,1024]{1,0:T(8,128)}, f32[128,128]{1,0:T(8,128)}, f32[128,128]{1,0:T(8,128)}, f32[1024,128]{1,0:T(8,128)},...) custom-call(f32[8,2,128,128]{3,2,1,0:T(8,128)} %get-tuple-element.25.keep_tot, ...), custom_call_target="tpu_custom_call" | custom-call | flops 67108864 | bytes 5242880 | tf_op jit(solution)/shard_map/pallas_call | solution.py:413
  72.7 0.0 copy-start
  72.7 0.7 copy-done
  73.4 0.6 reduce
Async XLA Ops:
  72.7 0.7 copy-start

commit v3 on v2

--- a/solution.py
+++ b/solution.py
@@ -210,6 +210,21 @@
     keep(tot, keep_tot)
     keep(moments, keep_moments)
     wall[s] = weights[...] - 0.01 * (0.9 * moments[...])
+    w_waits, w_y_waits = {}, []
+
+    def along_z(k):
+        w_waits[k] = group([(wall.at[s], wall.at[s], (((z + k) % Z) * Y + y, t))], wall.at[((z + Z - k) % Z) * Y + y])
+
+    def own_to_partner():
+        w_y_waits.append(group([(wall.at[s], wall.at[s], partner)], wall.at[z * Y + 1 - y]))
+
+    def forward(k):
+        c = (z + Z - k) % Z
+        w_waits[k]()
+        w_y_waits.append(group([(wall.at[c * Y + y], wall.at[c * Y + y], partner)], wall.at[c * Y + 1 - y]))
+
+    along_z(1)
+    along_z(3)
     vec = grad_v[...].astype(f32)
     length = moment_v.shape[1]
     vpart[...] = jnp.zeros_like(vpart)
@@ -224,13 +239,9 @@
         z_waits.append(group([(yrecv.at[c], zrecv.at[k], (c * Y + y, t))], zrecv.at[k]))
     y_waits[3]()
     total = yrecv[z] + tot[s]
-    w_waits = [group([(wall.at[s], wall.at[s], (((z + k) % Z) * Y + y, t))], wall.at[((z + Z - k) % Z) * Y + y]) for k in (1, 2, 3)]
-    w_y_waits = [group([(wall.at[s], wall.at[s], partner)], wall.at[z * Y + 1 - y])]
-
-    def forward(k):
-        c = (z + Z - k) % Z
-        w_waits[k - 1]()
-        w_y_waits.append(group([(wall.at[c * Y + y], wall.at[c * Y + y], partner)], wall.at[c * Y + 1 - y]))
+    own_to_partner()
+    forward(1)
+    forward(3)
 
     for k in range(Z - 1):
         z_waits[k]()
@@ -259,6 +270,8 @@
         scat_wait = scatter_shard(scat.at[a], got.at[a])
         xq[turn, t] = nt(factor_q, blk[0])
         xq_wait = spread_tensor(xq.at[turn])
+        if not last:
+            along_z(2)
         if turn:
             inverse_q, inverse_o = inverse_lower(gram_q), inverse_lower(gram_o)
         xq_wait()
@@ -281,7 +294,6 @@
         if last:
             pall[s] = left_q
             pall_wait = spread_shard(pall)
-            forward(2)
         q_wait()
         piece = scat[b, s]
         for k in range(SHARD - 1):
@@ -296,7 +308,8 @@
         xo[turn, t, RANK : 2 * RANK] = jnp.zeros((RANK, B), f32)
         xo[turn, t, RANK : 2 * RANK, 0:RANK] = nt(left_o, left_o)
         xo_wait = spread_tensor(xo.at[turn])
-        forward(3 if last else 1)
+        if not last:
+            forward(2)
         q_wait()
         factor_q = gath[b, 0 : RANK // 8].reshape(RANK, B)
         gram_q = gath[b, RANK // 8 : SHARD].reshape(RANK, B)[:, 0:RANK]
@@ -346,12 +359,14 @@
         copy.start()
         out.append(copy)
 
-    for load in loads:
+    for load in loads[:5]:
         load.wait()
     mq[...] = 0.9 * moments[0] + nn(pall[s].T, side_q[...])
     mo[...] = 0.9 * moments[1] + nn(side_o[...], fall[s])
     leave(mq, new_moment_q)
     leave(mo, new_moment_o)
+    for load in loads[5:]:
+        load.wait()
     for j in range(SHARD):
         rows = pl.ds(j * B, B)
         approx = nn(pall[j].T, side_q[...])
@@ -428,7 +443,7 @@
         compiler_params=pltpu.CompilerParams(vmem_limit_bytes=60 * 2**20),
         cost_estimate=pl.CostEstimate(flops=2**26, bytes_accessed=5 * 2**20, transcendentals=0),
     )(*kept)
-    return eq[None], eo[None], mq, mo, wq, wo, mv[0], wv[0]
+    return eq[None], eo[None], mq, mo, wq, wo, mv.reshape(-1), wv.reshape(-1)
 
 
 def solution(mesh):

time: 74.4 us -> 69.7 us (0.937)
  Pallas kernels: 72 us -> 67.3 us
    pallas_call x1, Pallas kernels: 66.8 us -> 62.2 us  [fast_local(): pl.pallas_call(kernel, out_shape=(shape(SHARD, 2, B, B), shape(SHARD, 2,...]
where the time goes in v3:
time: 69.7 us; the launch traced here: 69.3 us
  Pallas kernels  67.3 us (97%)
  local copies, waits for them, and re-layouts  0.71 us (1%)
    pallas_call x1, Pallas kernels, fast_local(): pl.pallas_call(kernel, out_shape=(shape(SHARD, 2, B, B), shape(SHARD, 2,...  62.2 us
    pallas_call x1, Pallas kernels, fast_local(): pl.pallas_call(finish, out_shape=(shape(SHARD * B, B), shape(B, SHARD * B...  5.13 us

profile of v3, /device:TPU:0, one launch (start us, length us, event | category | flops | bytes accessed | tf_op | source)
XLA Modules:
  0.0 69.3 jit_solution(3610082451076177009)
XLA Ops:
  0.6 62.2 %shard_map.188 = (f32[8,2,128,128]{3,2,1,0:T(8,128)}, f32[8,2,128,128]{3,2,1,0:T(8,128)}, f32[8,32,128]{2,1,0:T(8,128)}, f32[8,32,128]{2,1,0:T(8,128)}, f32[32,1...) custom-call(bf16[1024,128]{1,0:T(8,128)(2,1)} %bitcast.15, ...), custom_call_target="tpu_custom_call" | custom-call | flops 1073741824 | bytes 5242880 | tf_op jit(solution)/shard_map/pallas_call | solution.py:401
  62.8 5.1 %shard_map.189 = (f32[1024,128]{1,0:T(8,128)}, f32[128,1024]{1,0:T(8,128)}, f32[128,128]{1,0:T(8,128)}, f32[128,128]{1,0:T(8,128)}, f32[1024,128]{1,0:T(8,128)},...) custom-call(f32[8,2,128,128]{3,2,1,0:T(8,128)} %get-tuple-element.25.keep_tot, ...), custom_call_target="tpu_custom_call" | custom-call | flops 67108864 | bytes 5242880 | tf_op jit(solution)/shard_map/pallas_call | solution.py:428
  68.0 0.0 copy-start
  68.0 0.7 %copy-done = f32[1,3584]{1,0:T(1,128)S(1)} copy-done((f32[1,3584]{1,0:T(1,128)S(1)}, f32[1,3584]{1,0:T(1,128)}, u32[]{:S(2)}) %copy-start) | copy-done | bytes 14360
  68.7 0.6 reduce
Async XLA Ops:
  68.0 0.7 %copy-start = (f32[1,3584]{1,0:T(1,128)S(1)}, f32[1,3584]{1,0:T(1,128)}, u32[]{:S(2)}) copy-start(f32[1,3584]{1,0:T(1,128)} %get-tuple-element.41) | copy-start | bytes 43012

commit v4 on v3

--- a/solution.py
+++ b/solution.py
@@ -110,7 +110,7 @@
 RANK = 32
 B = 128
 VEC_PAD = 512
-SLOTS = 40
+SLOTS = 64
 f32 = jnp.float32
 
 
@@ -206,8 +206,11 @@
 
     partner = (z * Y + 1 - y, t)
     order = [(z + k) % Z for k in (1, 2, 3, 0)]
-    y_waits = [group([(tot.at[c * Y + 1 - y], yrecv.at[c], partner)], yrecv.at[c]) for c in order]
-    keep(tot, keep_tot)
+
+    def along_y(m, c):
+        return group([(tot.at[c * Y + 1 - y, m], yrecv.at[c, m], partner)], yrecv.at[c, m])
+
+    y_waits = {(0, c): along_y(0, order[c]) for c in range(2)}
     keep(moments, keep_moments)
     wall[s] = weights[...] - 0.01 * (0.9 * moments[...])
     w_waits, w_y_waits = {}, []
@@ -223,8 +226,37 @@
         w_waits[k]()
         w_y_waits.append(group([(wall.at[c * Y + y], wall.at[c * Y + y], partner)], wall.at[c * Y + 1 - y]))
 
+    def scatter_rows(i, part, square):
+        for j in range(RANK // 8):
+            scat[i, j] = part[8 * j : 8 * j + 8]
+            scat[i, j + RANK // 8] = jnp.zeros((8, B), f32)
+            if square is not None:
+                scat[i, j + RANK // 8, :, 0:RANK] = square[8 * j : 8 * j + 8]
+        return scatter_shard(scat.at[i], got.at[i])
+
+    def gather_rows(i, wait):
+        wait()
+        piece = scat[i, s]
+        for k in range(SHARD - 1):
+            piece = piece + got[i, k]
+        gath[i, s] = piece
+        return spread_shard(gath.at[i])
+
+    def rows_of(i, wait):
+        wait()
+        return gath[i, 0 : RANK // 8].reshape(RANK, B), gath[i, RANK // 8 : SHARD].reshape(RANK, B)[:, 0:RANK]
+
     along_z(1)
+    part_o = nt(so[:, 0:B], tot[0, 1])
+    for j in range(1, SHARD):
+        part_o = part_o + nt(so[:, j * B : (j + 1) * B], tot[j, 1])
+    o_wait = scatter_rows(0, part_o, None)
+    for c in (2, 3):
+        y_waits[0, c] = along_y(0, order[c])
+    for c in range(Z):
+        y_waits[1, c] = along_y(1, order[c])
     along_z(3)
+    keep(tot, keep_tot)
     vec = grad_v[...].astype(f32)
     length = moment_v.shape[1]
     vpart[...] = jnp.zeros_like(vpart)
@@ -232,22 +264,42 @@
     for j in range(SHARD):
         vpart[j, :, 0:length] = vec[:, j * length : (j + 1) * length]
     vector_wait = scatter_shard(vpart, vrecv)
-    z_waits = []
-    for k, c in enumerate(order[:3]):
-        y_waits[k]()
-        yrecv[c] = yrecv[c] + tot[c * Y + y]
-        z_waits.append(group([(yrecv.at[c], zrecv.at[k], (c * Y + y, t))], zrecv.at[k]))
-    y_waits[3]()
-    total = yrecv[z] + tot[s]
+    z_waits = {}
+    for m in range(2):
+        for k, c in enumerate(order[:3]):
+            y_waits[m, k]()
+            yrecv[c, m] = yrecv[c, m] + tot[c * Y + y, m]
+            z_waits[m, k] = group([(yrecv.at[c, m], zrecv.at[k, m], (c * Y + y, t))], zrecv.at[k, m])
+        if m == 0:
+            o_wait = gather_rows(0, o_wait)
+
+    def block(m):
+        y_waits[m, 3]()
+        total = yrecv[z, m] + tot[s, m]
+        for k in range(Z - 1):
+            z_waits[m, k]()
+            total = total + zrecv[k, m]
+        blk[m] = total
+
+    def to_tensor_q(turn, factor):
+        xq[turn, t] = nt(factor, blk[0])
+        return spread_tensor(xq.at[turn])
+
+    def to_tensor_o(turn, left):
+        xo[turn, t, 0:RANK] = nn(left, blk[1])
+        xo[turn, t, RANK : 2 * RANK] = jnp.zeros((RANK, B), f32)
+        xo[turn, t, RANK : 2 * RANK, 0:RANK] = nt(left, left)
+        return spread_tensor(xo.at[turn])
+
+    def summed(ref, turn, wait):
+        wait()
+        return ref[turn, 0] + ref[turn, 1] + ref[turn, 2] + ref[turn, 3]
+
     own_to_partner()
     forward(1)
+    block(0)
+    xq_wait = to_tensor_q(0, sq[...])
     forward(3)
-
-    for k in range(Z - 1):
-        z_waits[k]()
-        total = total + zrecv[k]
-    blk[...] = total
-
     vector_wait()
     vector_sum = vpart[s]
     for k in range(SHARD - 1):
@@ -255,84 +307,48 @@
     moment = 0.9 * moment_v[...] + vector_sum[:, 0:length] / SHARD
     new_moment_v[...] = moment
     vall[s, :, 0:length] = weight_v[...] - 0.01 * moment
+    left_q = summed(xq, 0, xq_wait)
+    q_wait = scatter_rows(1, nn(left_q, blk[0]), nt(left_q, left_q))
+    block(1)
+    left_o, _ = rows_of(0, o_wait)
+    xo_wait = to_tensor_o(0, left_o)
+    q_wait = gather_rows(1, q_wait)
     vall_wait = spread_shard(vall)
-
-    factor_q = sq[...]
-    factor_o = so[:, pl.ds(pl.multiple_of(s * B, B), B)]
-    inverse_q = inverse_o = None
-    for turn in range(ROUNDS):
-        last = turn == ROUNDS - 1
-        a, b = 2 * turn, 2 * turn + 1
-        part_o = nt(factor_o, blk[1])
-        for j in range(RANK // 8):
-            scat[a, j] = part_o[8 * j : 8 * j + 8]
-            scat[a, j + RANK // 8] = jnp.zeros((8, B), f32)
-        scat_wait = scatter_shard(scat.at[a], got.at[a])
-        xq[turn, t] = nt(factor_q, blk[0])
-        xq_wait = spread_tensor(xq.at[turn])
-        if not last:
-            along_z(2)
-        if turn:
-            inverse_q, inverse_o = inverse_lower(gram_q), inverse_lower(gram_o)
-        xq_wait()
-        left_q = xq[turn, 0] + xq[turn, 1] + xq[turn, 2] + xq[turn, 3]
-        if turn:
-            left_q = nn(inverse_q, left_q)
-        right_q = nn(left_q, blk[0])
-        square_q = nt(left_q, left_q)
-        for j in range(RANK // 8):
-            scat[b, j] = right_q[8 * j : 8 * j + 8]
-            scat[b, j + RANK // 8] = jnp.zeros((8, B), f32)
-            scat[b, j + RANK // 8, :, 0:RANK] = square_q[8 * j : 8 * j + 8]
-        q_wait = scatter_shard(scat.at[b], got.at[b])
-        scat_wait()
-        piece = scat[a, s]
-        for k in range(SHARD - 1):
-            piece = piece + got[a, k]
-        gath[a, s] = piece
-        o_wait = spread_shard(gath.at[a])
-        if last:
-            pall[s] = left_q
-            pall_wait = spread_shard(pall)
-        q_wait()
-        piece = scat[b, s]
-        for k in range(SHARD - 1):
-            piece = piece + got[b, k]
-        gath[b, s] = piece
-        q_wait = spread_shard(gath.at[b])
-        o_wait()
-        left_o = gath[a, 0 : RANK // 8].reshape(RANK, B)
-        if turn:
-            left_o = nn(inverse_o, left_o)
-        xo[turn, t, 0:RANK] = nn(left_o, blk[1])
-        xo[turn, t, RANK : 2 * RANK] = jnp.zeros((RANK, B), f32)
-        xo[turn, t, RANK : 2 * RANK, 0:RANK] = nt(left_o, left_o)
-        xo_wait = spread_tensor(xo.at[turn])
-        if not last:
-            forward(2)
-        q_wait()
-        factor_q = gath[b, 0 : RANK // 8].reshape(RANK, B)
-        gram_q = gath[b, RANK // 8 : SHARD].reshape(RANK, B)[:, 0:RANK]
-        xo_wait()
-        both = xo[turn, 0] + xo[turn, 1] + xo[turn, 2] + xo[turn, 3]
-        factor_o, gram_o = both[0:RANK], both[RANK : 2 * RANK, 0:RANK]
-
+    along_z(2)
+    both = summed(xo, 0, xo_wait)
+    factor_o, gram_o = both[0:RANK], both[RANK : 2 * RANK, 0:RANK]
+    o_wait = scatter_rows(2, nt(factor_o, blk[1]), None)
+    factor_q, gram_q = rows_of(1, q_wait)
+    xq_wait = to_tensor_q(1, factor_q)
+    o_wait = gather_rows(2, o_wait)
+    forward(2)
+    inverse_q, inverse_o = inverse_lower(gram_q), inverse_lower(gram_o)
+    left_q = nn(inverse_q, summed(xq, 1, xq_wait))
+    q_wait = scatter_rows(3, nn(left_q, blk[0]), nt(left_q, left_q))
+    left_o = nn(inverse_o, rows_of(2, o_wait)[0])
+    xo_wait = to_tensor_o(1, left_o)
+    q_wait = gather_rows(3, q_wait)
+    both = summed(xo, 1, xo_wait)
+    factor_o, gram_o = both[0:RANK], both[RANK : 2 * RANK, 0:RANK]
     fall[s] = factor_o
     fall_wait = spread_shard(fall)
+    pall[s] = left_q
+    pall_wait = spread_shard(pall)
+    factor_q, gram_q = rows_of(3, q_wait)
     inverse_q, inverse_o = inverse_lower(gram_q), inverse_lower(gram_o)
     side_q[...] = nn(inverse_q.T, nn(inverse_q, factor_q)) / SHARD
     side_o[...] = (nn(inverse_o.T, nn(inverse_o, left_o)) / SHARD).T
     keep(side_q, keep_q)
     keep(side_o, keep_o)
-    pall_wait()
-    keep(pall, keep_pall)
-    vall_wait()
-    keep(vall, keep_vall)
-    fall_wait()
-    keep(fall, keep_fall)
     for wait in w_y_waits:
         wait()
     keep(wall, keep_wall)
+    vall_wait()
+    keep(vall, keep_vall)
+    pall_wait()
+    keep(pall, keep_pall)
+    fall_wait()
+    keep(fall, keep_fall)
     for many, slot in sent:
         pltpu.make_async_copy(many, many, send_sem.at[slot]).wait()
     for copy in kept:

time: 69.7 us -> 66.1 us (0.948)
  Pallas kernels: 67.3 us -> 63.7 us
    pallas_call x1, Pallas kernels: 62.2 us -> 58.6 us  [fast_local(): pl.pallas_call(kernel, out_shape=(shape(SHARD, 2, B, B), shape(SHARD, 2,...]
where the time goes in v4:
time: 66.1 us; the launch traced here: 65.7 us
  Pallas kernels  63.7 us (96%)
  local copies, waits for them, and re-layouts  0.71 us (1%)
    pallas_call x1, Pallas kernels, fast_local(): pl.pallas_call(kernel, out_shape=(shape(SHARD, 2, B, B), shape(SHARD, 2,...  58.6 us
    pallas_call x1, Pallas kernels, fast_local(): pl.pallas_call(finish, out_shape=(shape(SHARD * B, B), shape(B, SHARD * B...  5.13 us

profile of v4, /device:TPU:0, one launch (start us, length us, event | category | flops | bytes accessed | tf_op | source)
XLA Modules:
  0.0 65.7 jit_solution(8574488008817192047)
XLA Ops:
  0.6 58.6 %shard_map.188 = (f32[8,2,128,128]{3,2,1,0:T(8,128)}, f32[8,2,128,128]{3,2,1,0:T(8,128)}, f32[8,32,128]{2,1,0:T(8,128)}, f32[8,32,128]{2,1,0:T(8,128)}, f32[32,1...) custom-call(bf16[1024,128]{1,0:T(8,128)(2,1)} %bitcast.15, ...), custom_call_target="tpu_custom_call" | custom-call | flops 1073741824 | bytes 5242880 | tf_op jit(solution)/shard_map/pallas_call | solution.py:417
  59.2 5.1 %shard_map.189 = (f32[1024,128]{1,0:T(8,128)}, f32[128,1024]{1,0:T(8,128)}, f32[128,128]{1,0:T(8,128)}, f32[128,128]{1,0:T(8,128)}, f32[1024,128]{1,0:T(8,128)},...) custom-call(f32[8,2,128,128]{3,2,1,0:T(8,128)} %get-tuple-element.25.keep_tot, ...), custom_call_target="tpu_custom_call" | custom-call | flops 67108864 | bytes 5242880 | tf_op jit(solution)/shard_map/pallas_call | solution.py:444
  64.4 0.0 copy-start
  64.4 0.7 %copy-done = f32[1,3584]{1,0:T(1,128)S(1)} copy-done((f32[1,3584]{1,0:T(1,128)S(1)}, f32[1,3584]{1,0:T(1,128)}, u32[]{:S(2)}) %copy-start) | copy-done | bytes 14360
  65.1 0.6 reduce
Async XLA Ops:
  64.4 0.7 %copy-start = (f32[1,3584]{1,0:T(1,128)S(1)}, f32[1,3584]{1,0:T(1,128)}, u32[]{:S(2)}) copy-start(f32[1,3584]{1,0:T(1,128)} %get-tuple-element.41) | copy-start | bytes 43012

commit v5 on v4

--- a/solution.py
+++ b/solution.py
@@ -246,7 +246,7 @@
         wait()
         return gath[i, 0 : RANK // 8].reshape(RANK, B), gath[i, RANK // 8 : SHARD].reshape(RANK, B)[:, 0:RANK]
 
-    along_z(1)
+    along_z(2)
     part_o = nt(so[:, 0:B], tot[0, 1])
     for j in range(1, SHARD):
         part_o = part_o + nt(so[:, j * B : (j + 1) * B], tot[j, 1])
@@ -255,7 +255,6 @@
         y_waits[0, c] = along_y(0, order[c])
     for c in range(Z):
         y_waits[1, c] = along_y(1, order[c])
-    along_z(3)
     keep(tot, keep_tot)
     vec = grad_v[...].astype(f32)
     length = moment_v.shape[1]
@@ -296,10 +295,9 @@
         return ref[turn, 0] + ref[turn, 1] + ref[turn, 2] + ref[turn, 3]
 
     own_to_partner()
-    forward(1)
+    forward(2)
     block(0)
     xq_wait = to_tensor_q(0, sq[...])
-    forward(3)
     vector_wait()
     vector_sum = vpart[s]
     for k in range(SHARD - 1):
@@ -314,14 +312,15 @@
     xo_wait = to_tensor_o(0, left_o)
     q_wait = gather_rows(1, q_wait)
     vall_wait = spread_shard(vall)
-    along_z(2)
+    along_z(1)
     both = summed(xo, 0, xo_wait)
     factor_o, gram_o = both[0:RANK], both[RANK : 2 * RANK, 0:RANK]
     o_wait = scatter_rows(2, nt(factor_o, blk[1]), None)
     factor_q, gram_q = rows_of(1, q_wait)
     xq_wait = to_tensor_q(1, factor_q)
     o_wait = gather_rows(2, o_wait)
-    forward(2)
+    along_z(3)
+    forward(1)
     inverse_q, inverse_o = inverse_lower(gram_q), inverse_lower(gram_o)
     left_q = nn(inverse_q, summed(xq, 1, xq_wait))
     q_wait = scatter_rows(3, nn(left_q, blk[0]), nt(left_q, left_q))
@@ -334,8 +333,10 @@
     fall_wait = spread_shard(fall)
     pall[s] = left_q
     pall_wait = spread_shard(pall)
+    forward(3)
+    inverse_o = inverse_lower(gram_o)
     factor_q, gram_q = rows_of(3, q_wait)
-    inverse_q, inverse_o = inverse_lower(gram_q), inverse_lower(gram_o)
+    inverse_q = inverse_lower(gram_q)
     side_q[...] = nn(inverse_q.T, nn(inverse_q, factor_q)) / SHARD
     side_o[...] = (nn(inverse_o.T, nn(inverse_o, left_o)) / SHARD).T
     keep(side_q, keep_q)

time: 66.1 us -> 64.5 us (0.976)
  Pallas kernels: 63.7 us -> 62.1 us
    pallas_call x1, Pallas kernels: 58.6 us -> 57 us  [fast_local(): pl.pallas_call(kernel, out_shape=(shape(SHARD, 2, B, B), shape(SHARD, 2,...]
where the time goes in v5:
time: 64.5 us; the launch traced here: 64.1 us
  Pallas kernels  62.1 us (96%)
  local copies, waits for them, and re-layouts  0.71 us (1%)
  between operations  0.66 us (1%)
    pallas_call x1, Pallas kernels, fast_local(): pl.pallas_call(kernel, out_shape=(shape(SHARD, 2, B, B), shape(SHARD, 2,...  57 us
    pallas_call x1, Pallas kernels, fast_local(): pl.pallas_call(finish, out_shape=(shape(SHARD * B, B), shape(B, SHARD * B...  5.13 us

profile of v5, /device:TPU:0, one launch (start us, length us, event | category | flops | bytes accessed | tf_op | source)
XLA Modules:
  0.0 64.1 jit_solution(3317289802730161346)
XLA Ops:
  0.6 57.0 %shard_map.188 = (f32[8,2,128,128]{3,2,1,0:T(8,128)}, f32[8,2,128,128]{3,2,1,0:T(8,128)}, f32[8,32,128]{2,1,0:T(8,128)}, f32[8,32,128]{2,1,0:T(8,128)}, f32[32,1...) custom-call(bf16[1024,128]{1,0:T(8,128)(2,1)} %bitcast.15, ...), custom_call_target="tpu_custom_call" | custom-call | flops 1073741824 | bytes 5242880 | tf_op jit(solution)/shard_map/pallas_call | solution.py:418
  57.6 5.1 %shard_map.189 = (f32[1024,128]{1,0:T(8,128)}, f32[128,1024]{1,0:T(8,128)}, f32[128,128]{1,0:T(8,128)}, f32[128,128]{1,0:T(8,128)}, f32[1024,128]{1,0:T(8,128)},...) custom-call(f32[8,2,128,128]{3,2,1,0:T(8,128)} %get-tuple-element.25.keep_tot, ...), custom_call_target="tpu_custom_call" | custom-call | flops 67108864 | bytes 5242880 | tf_op jit(solution)/shard_map/pallas_call | solution.py:445
  62.8 0.0 copy-start
  62.8 0.7 %copy-done = f32[1,3584]{1,0:T(1,128)S(1)} copy-done((f32[1,3584]{1,0:T(1,128)S(1)}, f32[1,3584]{1,0:T(1,128)}, u32[]{:S(2)}) %copy-start) | copy-done | bytes 14360
  63.5 0.6 reduce
Async XLA Ops:
  62.8 0.7 %copy-start = (f32[1,3584]{1,0:T(1,128)S(1)}, f32[1,3584]{1,0:T(1,128)}, u32[]{:S(2)}) copy-start(f32[1,3584]{1,0:T(1,128)} %get-tuple-element.41) | copy-start | bytes 43012
